TPU v7x, 32 devices: a whole 2x2x4 slice. The times are simulated.
32 devices in a mesh: narrow: 4 (over y, core), wide: 8 (over z, x).
Axes of the slice: x: 2, y: 2, z: 4, core: 2. Of those that a mesh axis runs over, the one named last changes fastest.
Arguments:
- inputs: bfloat16 [256, 8, 100], P('wide'), may hold values from -6 to 6
- cotangent: bfloat16 [256, 8, 10], P('wide'), may hold values from -6 to 6
- step_mask: int32 [256, 8], P('wide'), may hold values 0 or 1
- washout: int32 [256], P('wide'), may hold values from 0 to 1
- lengths: int32 [256], P('wide'), may hold values from 4 to 8
- leak_groups: int32 [2, 4, 2048], P(None, 'narrow'), may hold values 0 or 1
- leak_two: float32 [4], P('narrow'), may hold values from 0.03 to 0.3
- w_one: bfloat16 [4, 2048, 2048], P('narrow'), may hold values from -0.125 to 0.125
- v_one: bfloat16 [4, 100, 2048], P('narrow'), may hold values from -0.625 to 0.625
- v_two: bfloat16 [4, 2048, 2048], P('narrow'), may hold values from -0.25 to 0.25
- w_two: bfloat16 [4, 2048, 2048], P('narrow'), may hold values from -0.125 to 0.125
- w_out: bfloat16 [8192, 10], P('narrow'), may hold values from -0.0625 to 0.0625
- b_out: float32 [10], replicated, may hold values from -4 to 4
Outputs:
- output: float32 [256, 8, 10], P('wide', 'narrow')
- input_grad: float32 [256, 8, 100], P('wide')
- grad_w_one: float32 [4, 2048, 2048], P('narrow', None, 'wide')
- grad_v_one: float32 [4, 100, 2048], P('narrow', None, 'wide')
- grad_v_two: float32 [4, 2048, 2048], P('narrow', None, 'wide')
- grad_w_two: float32 [4, 2048, 2048], P('narrow', None, 'wide')
- grad_w_out: float32 [8192, 10], P('narrow')
- grad_b_out: float32 [10], replicated
All inputs are finite; a program needn't handle non-finite values. No bound on the sum of `step_mask` or of `leak_groups` on one device may be relied on, other than what follows from the above.
Results may differ from a plain program's by a relative error of at most 0.0055.
Values may be sent and summed in bfloat16 or wider, within the bound.
No kernel may reach another device: no remote copies, remote signals or barrier semaphores. Data moves between devices by JAX's collectives and lax.ppermute only.
A program may use at most 192 MiB of HBM per device.

v0:
```python
import jax
import jax.numpy as jnp
from jax import lax
from jax.sharding import PartitionSpec as P


def feature_grad(grads, values, valid, mean, inv, count, sum_g, sum_gx):
    slope = -0.5 * inv * inv * inv * (sum_gx - mean * sum_g)
    shift = -inv * sum_g - 2.0 * mean * slope
    result = inv * grads + valid[:, :, None] * (shift + 2.0 * values * slope) / count
    return result.astype(jnp.bfloat16)


def statistics(values, valid):
    weights = valid[:, :, None]
    return (
        jnp.sum(weights * values, axis=(0, 1)),
        jnp.sum(weights * values * values, axis=(0, 1)),
        jnp.sum(valid),
    )


def normalize(values, totals):
    mean = totals[0] / totals[2]
    inv = lax.rsqrt(totals[1] / totals[2] - mean * mean + 1e-05)
    return (mean, inv, ((values - mean) * inv).astype(jnp.bfloat16))


def back_layer(extra, pre, rate, weight):

    def back_step(carry, items):
        ext_now, pre_now = items
        grad_h = ext_now + carry
        slope = 1.0 - jnp.square(jnp.tanh(pre_now))
        grad_p = (grad_h * rate * slope).astype(jnp.bfloat16)
        carry = (1.0 - rate) * grad_h + lax.dot_general(
            grad_p, weight, (((1,), (1,)), ((), ())), preferred_element_type=jnp.float32
        )
        return (carry, grad_p)

    start = jnp.zeros(extra.shape[1:], jnp.float32)
    final, grad_pre = lax.scan(back_step, start, (extra, pre), reverse=True)
    return grad_pre


def shifted(states):
    return jnp.concatenate([jnp.zeros_like(states[:1]), states[:-1]], axis=0)


def outer_sum(left, right):
    return jnp.einsum("tbr,tbq->rq", left, right, preferred_element_type=jnp.float32)


def on_device(
    inputs,
    cotangent,
    step_mask,
    washout,
    lengths,
    leak_groups,
    leak_two,
    w_one,
    v_one,
    v_two,
    w_two,
    w_out,
    b_out,
):
    rates = jnp.where(leak_groups == 0, jnp.float32(0.3), leak_two[None, :, None])
    rate_one = rates[0, 0]
    rate_two = rates[1, 0]
    input_weight_first = w_one[0]
    recurrent_weight_first = v_one[0]
    recurrent_weight_second = v_two[0]
    input_weight_second = w_two[0]
    seqs, steps, width_in = inputs.shape
    units = input_weight_first.shape[0]
    position = jnp.arange(steps, dtype=jnp.int32)[None, :]
    valid_rows = (
        (step_mask == 1) & (position >= washout[:, None]) & (position < lengths[:, None])
    ).astype(jnp.float32)
    valid_tm = jnp.transpose(valid_rows, (1, 0))
    series = jnp.transpose(inputs, (1, 0, 2))

    def advance(carry, current_input):
        h_one, h_two, leaky_state_first, leaky_state_second = carry
        preactivation_first = jnp.dot(
            leaky_state_first, input_weight_first, preferred_element_type=jnp.float32
        ) + jnp.dot(current_input, recurrent_weight_first, preferred_element_type=jnp.float32)
        h_one = (1.0 - rate_one) * h_one + rate_one * jnp.tanh(preactivation_first)
        leaky_state_first = h_one.astype(jnp.bfloat16)
        preactivation_second = jnp.dot(
            leaky_state_second, input_weight_second, preferred_element_type=jnp.float32
        ) + jnp.dot(leaky_state_first, recurrent_weight_second, preferred_element_type=jnp.float32)
        h_two = (1.0 - rate_two) * h_two + rate_two * jnp.tanh(preactivation_second)
        leaky_state_second = h_two.astype(jnp.bfloat16)
        return (
            (h_one, h_two, leaky_state_first, leaky_state_second),
            (preactivation_first, preactivation_second, leaky_state_first, leaky_state_second),
        )

    zero_float = jnp.zeros((seqs, units), jnp.float32)
    zero_low = jnp.zeros((seqs, units), jnp.bfloat16)
    final, kept = lax.scan(advance, (zero_float, zero_float, zero_low, zero_low), series)
    preactivation_first, preactivation_second, low_one, low_two = kept
    narrow_count = lax.axis_size("narrow")
    piece = steps // narrow_count
    member = lax.axis_index("narrow")
    dy_tm = jnp.transpose(cotangent, (1, 0, 2))
    dy_tm = jnp.where(valid_tm[:, :, None] > 0, dy_tm, jnp.zeros_like(dy_tm))
    feats = lax.all_to_all(low_two, "narrow", split_axis=0, concat_axis=2, tiled=True)
    head = lax.all_gather(w_out, "narrow", axis=0, tiled=True)
    valid_part = lax.dynamic_slice_in_dim(valid_tm, member * piece, piece, 0)
    dy_part = lax.dynamic_slice_in_dim(dy_tm, member * piece, piece, 0)
    values = feats.astype(jnp.float32)
    totals = lax.psum(statistics(values, valid_part), ("narrow", "wide"))
    mean, inv, normed = normalize(values, totals)
    out_tm = jnp.dot(normed, head, preferred_element_type=jnp.float32) + b_out
    grads = jnp.einsum("pbo,fo->pbf", dy_part, head, preferred_element_type=jnp.float32)
    sum_g = jnp.sum(grads, axis=(0, 1))
    sum_gx = jnp.sum(grads * values, axis=(0, 1))
    head_grad = jnp.einsum("pbf,pbo->fo", normed, dy_part, preferred_element_type=jnp.float32)
    bias_grad = jnp.sum(dy_part.astype(jnp.float32), axis=(0, 1))
    sum_g, sum_gx, head_grad, bias_grad = lax.psum(
        (sum_g, sum_gx, head_grad, bias_grad), ("narrow", "wide")
    )
    dfeat = feature_grad(grads, values, valid_part, mean, inv, totals[2], sum_g, sum_gx)
    dfeat = lax.all_to_all(dfeat, "narrow", split_axis=2, concat_axis=0, tiled=True)
    own_head = lax.dynamic_slice_in_dim(head_grad, member * units, units, 0)
    output = jnp.transpose(out_tm, (1, 0, 2))
    grad_pre_two = back_layer(
        dfeat.astype(jnp.float32), preactivation_second, rate_two, input_weight_second
    )
    upper_cols = lax.all_to_all(grad_pre_two, "wide", split_axis=2, concat_axis=1, tiled=True)
    part_one = lax.all_gather(low_one, "wide", axis=1, tiled=True)
    part_two = lax.all_gather(low_two, "wide", axis=1, tiled=True)
    cols = upper_cols
    sent_vb = outer_sum(part_one, cols)
    sent_wb = outer_sum(shifted(part_two), cols)
    into_one = jnp.einsum(
        "tbq,rq->tbr", grad_pre_two, recurrent_weight_second, preferred_element_type=jnp.float32
    )
    grad_pre_one = back_layer(into_one, preactivation_first, rate_one, input_weight_first)
    input_part = jnp.einsum(
        "tbq,iq->bti", grad_pre_one, recurrent_weight_first, preferred_element_type=jnp.float32
    )
    input_grad = lax.psum(input_part, "narrow")
    lower_cols = lax.all_to_all(grad_pre_one, "wide", split_axis=2, concat_axis=1, tiled=True)
    part_one = lax.all_gather(low_one, "wide", axis=1, tiled=True)
    part_in = lax.all_gather(series, "wide", axis=1, tiled=True)
    cols = lower_cols
    sent_wa = outer_sum(shifted(part_one), cols)
    sent_va = jnp.einsum("tbi,tbq->iq", part_in, cols, preferred_element_type=jnp.float32)
    return (
        output,
        input_grad,
        sent_wa[None],
        sent_va[None],
        sent_vb[None],
        sent_wb[None],
        own_head,
        bias_grad,
    )


def solution(mesh):
    in_specs = (
        P("wide", None, None),
        P("wide", None, None),
        P("wide", None),
        P("wide"),
        P("wide"),
        P(None, "narrow", None),
        P("narrow"),
        P("narrow", None, None),
        P("narrow", None, None),
        P("narrow", None, None),
        P("narrow", None, None),
        P("narrow", None),
        P(),
    )
    out_specs = (
        P("wide", "narrow", None),
        P("wide", None, None),
        P("narrow", None, "wide"),
        P("narrow", None, "wide"),
        P("narrow", None, "wide"),
        P("narrow", None, "wide"),
        P("narrow", None),
        P(),
    )
    return jax.shard_map(
        on_device, mesh=mesh, in_specs=in_specs, out_specs=out_specs, check_vma=False
    )
```

profile of v0, /device:TPU:0, one launch (start us, length us, event | category | flops | bytes accessed | tf_op | source)
XLA Modules:
  0.0 715.1 jit_solution(11959357410567081167)
XLA Ops:
  12.6 94.2 %while.59 = (s32[]{:T(128)}, f32[32,2048]{1,0:T(8,128)S(1)}, f32[32,2048]{1,0:T(8,128)S(1)}, bf16[32,2048]{1,0:T(8,128)(2,1)S(1)}, bf16[32,2048]{1,0:T(8,128)(2,...) while((s32[]{:T(128)}, f32[32,2048]{1,0:T(8,128)S(1)}, ...), condition=%wide.region_1.2_spmd.clone, body=%wide.region_0.1_spmd.clone.sunk | while | flops 819335168 | bytes 80586552 | solution.py:104
  111.2 17.2 %all_gather.13 = bf16[8192,10]{0,1:T(8,128)(2,1)S(1)} all-gather(bf16[2048,10]{0,1:T(8,128)(2,1)S(1)} %copy-done.8), channel_id=1, replica_groups=mesh['narrow'=4,'wide'=8] {'narrow'}, dimensions={0}, use_global_device_ids=true | all-gather | bytes 204800 | tf_op jit(solution)/shard_map/all_gather | solution.py:112
  141.4 44.6 %all-reduce.10 = (f32[8192]{0:T(1024)S(1)}, f32[]{:T(128)}, f32[8192]{0:T(1024)S(1)}, f32[8192]{0:T(1024)S(1)}, f32[8192]{0:T(1024)S(1)}, /*index=5*/f32[10]{0:T(128)}) all-reduce(f32[8192]{0:T(1024)S(1)} %bitcast.234, f32[]{:T(128)} %get-tuple-element.656, ...), channel_id=1, replica_groups=mesh['narrow'=4,'wide'=8] {'narrow','wide'}, use_global_device_ids=true, to_apply=%region_3.4 | all-reduce | flops 32779 | bytes 262232 | tf_op jit(solution)/shard_map/psum | solution.py:116
  191.0 9.2 %copy.36 = bf16[2,32,8192]{1,0,2:T(2,128)(2,1)} copy(bf16[2,32,8192]{2,1,0:T(8,128)(2,1)} %add_convert_fusion) | data formatting | bytes 2097152 | tf_op jit(solution)/shard_map/convert_element_type | solution.py:11
  200.2 6.4 reshape.80
  212.8 12.9 %all-to-all-done.1 = bf16[4,2,65536]{2,1,0:T(2,128)(2,1)} async-done(((bf16[4,2,65536]{2,1,0:T(2,128)(2,1)}), bf16[4,2,65536]{2,1,0:T(2,128)(2,1)}, u32[]{:S(2)}, u32[]{:S(2)}) %all-to-all-start.1) | async-done | bytes 1048608 | tf_op jit(solution)/shard_map/all_to_all | solution.py:128
  230.9 6.6 convert_bitcast_fusion
  237.5 11.7 %copy.37 = f32[4,2,32,2048]{3,2,1,0:T(8,128)} copy(f32[4,2,32,2048]{2,1,3,0:T(2,128)} %convert_bitcast_fusion) | data formatting | bytes 4194304 | tf_op jit(solution)/shard_map/convert_element_type | solution.py:132
  250.3 62.2 %while.60 = (s32[]{:T(128)}, f32[32,2048]{1,0:T(8,128)S(1)}, bf16[8,32,2048]{2,1,0:T(8,128)(2,1)}, f32[2048]{0:T(1024)S(1)}, f32[8,32,2048]{2,1,0:T(8,128)}, /*i...) while((s32[]{:T(128)}, f32[32,2048]{1,0:T(8,128)S(1)}, ...), condition=%wide.region_13.14_spmd.clone, body=%wide.region_12.13_spmd.clone.sunk | while | flops 269158400 | bytes 10387604 | solution.py:42
  252.0 6.0 convolution_add_fusion.7
  259.8 6.0 convolution_add_fusion.7
  267.6 6.0 convolution_add_fusion.7
  275.4 6.0 convolution_add_fusion.7
  283.1 6.0 convolution_add_fusion.7
  290.9 6.0 convolution_add_fusion.7
  298.7 6.0 convolution_add_fusion.7
  306.4 6.0 convolution_add_fusion.7
  312.4 7.4 %fusion.17 = f32[8,32,2048]{2,1,0:T(8,128)} fusion(bf16[8,32,2048]{2,1,0:T(8,128)(2,1)} %get-tuple-element.425, bf16[1,2048,2048]{2,1,0:T(8,128)(2,1)} %bitcast.199), kind=kOutput, calls=%fused_computation.39 | convolution fusion | flops 2147483648 | bytes 11534336 | tf_op jit(solution)/shard_map/tbq,rq->tbr/dot_general | solution.py:140
  320.9 62.0 %while.61 = (s32[]{:T(128)}, f32[32,2048]{1,0:T(8,128)S(1)}, bf16[8,32,2048]{2,1,0:T(8,128)(2,1)}, f32[2048]{0:T(1024)S(1)}, f32[8,32,2048]{2,1,0:T(8,128)}, /*i...) while((s32[]{:T(128)}, f32[32,2048]{1,0:T(8,128)S(1)}, ...), condition=%wide.region_15.16_spmd.clone, body=%wide.region_14.15_spmd.clone.sunk | while | flops 269158400 | bytes 10387604 | solution.py:42
  322.7 6.0 convolution_add_fusion.8
  330.4 6.0 convolution_add_fusion.8
  338.2 6.0 convolution_add_fusion.8
  361.5 6.0 convolution_add_fusion.8
  377.0 6.0 convolution_add_fusion.8
  395.5 7.9 %reshape.84 = bf16[8,2,32768]{2,1,0:T(2,128)(2,1)} reshape(bf16[2048,8,32]{2,1,0:T(8,128)(2,1)} %bitcast.204) | data formatting | bytes 2097152
  412.0 7.8 %reshape.82 = bf16[8,2,32768]{2,1,0:T(2,128)(2,1)} reshape(bf16[2048,8,32]{2,1,0:T(8,128)(2,1)} %bitcast.205) | data formatting | bytes 2097152
  419.9 35.7 %all-to-all-done.3 = bf16[8,2,32768]{2,1,0:T(2,128)(2,1)} async-done(((bf16[8,2,32768]{2,1,0:T(2,128)(2,1)}), bf16[8,2,32768]{2,1,0:T(2,128)(2,1)}, u32[]{:S(2)}, u32[]{:S(2)}) %all-to-all-start.3) | async-done | bytes 1048608 | tf_op jit(solution)/shard_map/all_to_all | solution.py:134
  459.1 83.5 %all_gather.15 = bf16[8,256,100]{2,1,0:T(8,128)(2,1)} all-gather(bf16[8,32,100]{2,1,0:T(8,128)(2,1)S(1)} %get-tuple-element.1043), channel_id=1, replica_groups=mesh['narrow'=4,'wide'=8] {'wide'}, dimensions={1}, use_global_device_ids=true | all-gather | bytes 460800 | tf_op jit(solution)/shard_map/all_gather | solution.py:150
  547.3 7.1 reshape.85
  575.3 19.8 %fusion.23 = f32[1,2048,256]{2,1,0:T(8,128)} fusion(bf16[8,256,256]{2,1,0:T(8,128)(2,1)S(1)} %bitcast.212, bf16[7,256,2048]{2,0,1:T(8,128)(2,1)} %bitcast.239), kind=kOutput, calls=%fused_computation.47 | convolution fusion | flops 1879048192 | bytes 10485760 | tf_op jit(solution)/shard_map/tbr,tbq->rq/dot_general | solution.py:51
  595.1 87.9 %all-gather.5.cloned.1.call-done = bf16[8,256,2048]{2,0,1:T(8,128)(2,1)} async-done(((bf16[8,32,2048]{2,0,1:T(8,128)(2,1)}), bf16[8,256,2048]{2,0,1:T(8,128)(2,1)}) %all-gather.5.cloned.1.call-update) | async-done | bytes 8388624 | tf_op jit(solution)/shard_map/all_gather | solution.py:136
  683.1 19.7 %fusion.26 = f32[1,2048,256]{2,1,0:T(8,128)} fusion(bf16[8,256,256]{2,1,0:T(8,128)(2,1)S(1)} %bitcast.230, bf16[7,256,2048]{2,0,1:T(8,128)(2,1)} %bitcast.240), kind=kOutput, calls=%fused_computation.48 | convolution fusion | flops 1879048192 | bytes 10485760 | tf_op jit(solution)/shard_map/tbr,tbq->rq/dot_general | solution.py:51
  (266 shorter events, 234.8 us)
Async XLA Ops:
  12.6 6.0 slice-start
  12.6 6.0 slice-start.1
  24.3 6.0 slice-start
  24.3 6.0 slice-start.1
  36.1 6.0 slice-start
  36.1 6.0 slice-start.1
  47.9 6.0 slice-start
  47.9 6.0 slice-start.1
  59.7 6.0 slice-start
  59.7 6.0 slice-start.1
  71.4 6.0 slice-start
  71.4 6.0 slice-start.1
  83.2 6.0 slice-start
  83.2 6.0 slice-start.1
  95.0 6.0 slice-start
  95.0 6.0 slice-start.1
  106.7 21.7 %copy-start.10 = (s32[32,8]{0,1:T(8,128)S(1)}, s32[32,8]{0,1:T(8,128)}, u32[]{:S(2)}) copy-start(s32[32,8]{0,1:T(8,128)} %param.21) | copy-start | bytes 3076
  106.7 21.7 %copy-start.11 = (s32[32]{0:T(128)S(1)}, s32[32]{0:T(128)}, u32[]{:S(2)}) copy-start(s32[32]{0:T(128)} %param.23) | copy-start | bytes 388
  106.8 21.7 %copy-start.12 = (s32[32]{0:T(128)S(1)}, s32[32]{0:T(128)}, u32[]{:S(2)}) copy-start(s32[32]{0:T(128)} %param.22) | copy-start | bytes 388
  106.8 22.5 %all-to-all-start = ((bf16[8,32,2048]{2,1,0:T(8,128)(2,1)}), bf16[8,32,2048]{2,1,0:T(8,128)(2,1)}, u32[]{:S(2)}, u32[]{:S(2)}) async-start(bf16[8,32,2048]{2,1,0:T(8,128)(2,1)} %get-tuple-element.423), calls=%async_computation | async-start | bytes 2097152 | tf_op jit(solution)/shard_map/all_to_all | solution.py:111
  111.2 28.4 %copy-start.7 = (bf16[32,8,10]{0,2,1:T(8,128)(2,1)}, bf16[32,8,10]{0,2,1:T(8,128)(2,1)S(1)}, u32[]{:S(2)}) copy-start(bf16[32,8,10]{0,2,1:T(8,128)(2,1)S(1)} %copy.74) | copy-start | bytes 15364
  206.6 19.1 %all-to-all-start.1 = ((bf16[4,2,65536]{2,1,0:T(2,128)(2,1)}), bf16[4,2,65536]{2,1,0:T(2,128)(2,1)}, u32[]{:S(2)}, u32[]{:S(2)}) async-start(bf16[4,2,65536]{2,1,0:T(2,128)(2,1)} %reshape.80), calls=%async_computation.1 | async-start | bytes 2097152 | tf_op jit(solution)/shard_map/all_to_all | solution.py:128
  210.8 333.2 %all-reduce.9.cloned.1.call-start = ((), (), s32[]{:S(2)}) async-start(), calls=%async_computation.7 | async-start | bytes 1048576 | tf_op jit(solution)/shard_map/psum | solution.py:124
  212.8 332.9 %all-reduce.7.cloned.1.call-start = ((), (), s32[]{:S(2)}) async-start(), calls=%async_computation.4 | async-start | bytes 262144 | tf_op jit(solution)/shard_map/psum | solution.py:147
  385.3 190.0 %all-gather.3.cloned.1.call-start = ((), (), s32[]{:S(2)}) async-start(), calls=%async_computation.5 | async-start | bytes 9437184 | tf_op jit(solution)/shard_map/all_gather | solution.py:149
  388.1 295.0 %all-gather.5.cloned.1.call-start = ((), (), s32[]{:S(2)}) async-start(), calls=%async_computation.6 | async-start | bytes 9437184 | tf_op jit(solution)/shard_map/all_gather | solution.py:136
  403.3 52.2 %all-to-all-start.3 = ((bf16[8,2,32768]{2,1,0:T(2,128)(2,1)}), bf16[8,2,32768]{2,1,0:T(2,128)(2,1)}, u32[]{:S(2)}, u32[]{:S(2)}) async-start(bf16[8,2,32768]{2,1,0:T(2,128)(2,1)} %reshape.84), calls=%async_computation.3 | async-start | bytes 2097152 | tf_op jit(solution)/shard_map/all_to_all | solution.py:134
  419.9 122.8 %copy-start.13 = (f32[10]{0:T(128)S(1)}, f32[10]{0:T(128)}, u32[]{:S(2)}) copy-start(f32[10]{0:T(128)} %param.31) | copy-start | bytes 124
  455.6 109.6 %all-to-all-start.2 = ((bf16[8,2,32768]{2,1,0:T(2,128)(2,1)}), bf16[8,2,32768]{2,1,0:T(2,128)(2,1)S(1)}, u32[]{:S(2)}, u32[]{:S(2)}) async-start(bf16[8,2,32768]{2,1,0:T(2,128)(2,1)} %reshape.82), calls=%async_computation.2 | async-start | bytes 2097152 | tf_op jit(solution)/shard_map/all_to_all | solution.py:148
  575.3 107.8 %copy-start.6 = (bf16[8,32,8,256]{3,1,2,0:T(8,128)(2,1)S(1)}, bf16[8,32,8,256]{3,1,2,0:T(8,128)(2,1)}, u32[]{:S(2)}) copy-start(bf16[8,32,8,256]{3,1,2,0:T(8,128)(2,1)} %copy.43) | copy-start | bytes 3145732
  683.1 19.7 %copy-start.5 = (bf16[8,32,8,256]{3,0,1,2:T(8,128)(2,1)S(1)}, bf16[8,32,8,256]{3,0,1,2:T(8,128)(2,1)}, u32[]{:S(2)}) copy-start(bf16[8,32,8,256]{3,0,1,2:T(8,128)(2,1)} %copy.52) | copy-start | bytes 3145732
  683.1 19.7 %copy-start.14 = (bf16[8,256,2048]{2,0,1:T(8,128)(2,1)S(1)}, bf16[8,256,2048]{2,0,1:T(8,128)(2,1)}, u32[]{:S(2)}) copy-start(bf16[8,256,2048]{2,0,1:T(8,128)(2,1)} %all-gather.3.cloned.1.call-done) | copy-start | bytes 25165828
  (23 other events, 69.5 us)
Sparse Core Ops, SparseCore 0:
  216.9 127.4 all-reduce.8
  385.4 29.5 all-reduce.6
Sparse Core Ops, SparseCore 1:
  388.5 169.6 all-gather.2
  560.1 123.0 all-gather.4
where the time goes:
time: 725 us; the launch traced here: 715 us
  matrix products  233 us (32%)
  blocking collectives  145 us (20%)
  waiting for transfers between devices  137 us (19%)
  local copies, waits for them, and re-layouts  120 us (17%)
  other arithmetic  46.4 us (6%)
  starting transfers between devices  16.9 us (2%)
  between operations  16.7 us (2%)
    dot_general x16, matrix products, back_step(): lax.dot_general(grad_p, weight, (((1,), (1,)), ((), ())), preferred_eleme...  95.6 us
    all_gather x1, waiting for transfers between devices, on_device(): part_two = lax.all_gather(low_two, 'wide', axis=1, tiled=True)  87.9 us
    all_gather x1, blocking collectives, on_device(): part_in = lax.all_gather(series, 'wide', axis=1, tiled=True)  83.5 us
    psum x1, blocking collectives, on_device(): totals = lax.psum(statistics(values, valid_part), ('narrow', 'wide'))  44.6 us
    dot_general x3, matrix products, outer_sum(): jnp.einsum('tbr,tbq->rq', left, right, preferred_element_type=jnp.float32)  44.3 us
    unnamed x43, local copies, waits for them, and re-layouts  42.8 us
    dot_general x8, matrix products, advance(): jnp.dot(leaky_state_first, input_weight_first, preferred_element_type=jnp...  40.6 us
    all_to_all x1, waiting for transfers between devices, on_device(): lax.all_to_all(grad_pre_two, 'wide', split_axis=2, concat_axis=1, tiled=T...  35.7 us
  transfers between devices with their start and end apart: 8, of which 3 were waited for; matrix products, arithmetic and copies ran while one was open for 34% of the time, Pallas kernels for 0%

commit v1 on v0

--- a/solution.py
+++ b/solution.py
@@ -113,7 +113,9 @@
     valid_part = lax.dynamic_slice_in_dim(valid_tm, member * piece, piece, 0)
     dy_part = lax.dynamic_slice_in_dim(dy_tm, member * piece, piece, 0)
     values = feats.astype(jnp.float32)
-    totals = lax.psum(statistics(values, valid_part), ("narrow", "wide"))
+    totals = lax.psum(
+        lax.psum(statistics(values, valid_part), axis_name="wide"), axis_name="narrow"
+    )
     mean, inv, normed = normalize(values, totals)
     out_tm = jnp.dot(normed, head, preferred_element_type=jnp.float32) + b_out
     grads = jnp.einsum("pbo,fo->pbf", dy_part, head, preferred_element_type=jnp.float32)

time: 725 us -> 806 us (1.11)
  waiting for transfers between devices: 137 us -> 197 us
  local copies, waits for them, and re-layouts: 120 us -> 130 us
    psum x1 -> x2, waiting for transfers between devices: 0.01 us -> 67.6 us  [on_device(): lax.psum((sum_g, sum_gx, head_grad, bias_grad), ('narrow', 'wide'))]
    all_to_all x1, local copies, waits for them, and re-layouts: 4.47 us -> 13.2 us  [on_device(): lax.all_to_all(grad_pre_one, 'wide', split_axis=2, concat_axis=1, tiled=T...]
    all_gather x1, waiting for transfers between devices: 87.9 us -> 79.5 us  [on_device(): part_two = lax.all_gather(low_two, 'wide', axis=1, tiled=True)]
    psum x1 -> x2, blocking collectives: 44.6 us -> 52.7 us  [the longest x1 40.2 us: on_device(): lax.psum(statistics(values, valid_part), axis_name='wide')]
    unnamed x43 -> x46, local copies, waits for them, and re-layouts: 42.8 us -> 43.5 us
  transfers between devices with their start and end apart: 8 -> 9, of which waited for: 3 -> 4; matrix products, arithmetic and copies ran while one was open for 34% -> 32% of each run, Pallas kernels for 0% -> 0%
where the time goes in v1:
time: 806 us; the launch traced here: 795 us
  matrix products  233 us (29%)
  waiting for transfers between devices  197 us (24%)
  blocking collectives  153 us (19%)
  local copies, waits for them, and re-layouts  130 us (16%)
  other arithmetic  48.4 us (6%)
  starting transfers between devices  17.8 us (2%)
  between operations  16.6 us (2%)
    dot_general x16, matrix products, back_step(): lax.dot_general(grad_p, weight, (((1,), (1,)), ((), ())), preferred_eleme...  95.5 us
    all_gather x1, blocking collectives, on_device(): part_in = lax.all_gather(series, 'wide', axis=1, tiled=True)  83.1 us
    all_gather x1, waiting for transfers between devices, on_device(): part_two = lax.all_gather(low_two, 'wide', axis=1, tiled=True)  79.5 us
    psum x2, waiting for transfers between devices, on_device(): lax.psum((sum_g, sum_gx, head_grad, bias_grad), ('narrow', 'wide'))  67.6 us
    dot_general x3, matrix products, outer_sum(): jnp.einsum('tbr,tbq->rq', left, right, preferred_element_type=jnp.float32)  44.1 us
    unnamed x46, local copies, waits for them, and re-layouts  43.5 us
    dot_general x8, matrix products, advance(): jnp.dot(leaky_state_first, input_weight_first, preferred_element_type=jnp...  40.6 us
    psum x1, blocking collectives, on_device(): lax.psum(statistics(values, valid_part), axis_name='wide')  40.2 us
  transfers between devices with their start and end apart: 9, of which 4 were waited for; matrix products, arithmetic and copies ran while one was open for 32% of the time, Pallas kernels for 0%

profile of v1, /device:TPU:0, one launch (start us, length us, event | category | flops | bytes accessed | tf_op | source)
XLA Modules:
  0.0 795.3 jit_solution(13583776006990727544)
XLA Ops:
  12.6 94.1 %while.59 = (s32[]{:T(128)}, f32[32,2048]{1,0:T(8,128)S(1)}, f32[32,2048]{1,0:T(8,128)S(1)}, bf16[32,2048]{1,0:T(8,128)(2,1)S(1)}, bf16[32,2048]{1,0:T(8,128)(2,...) while((s32[]{:T(128)}, f32[32,2048]{1,0:T(8,128)S(1)}, ...), condition=%wide.region_1.2_spmd.clone, body=%wide.region_0.1_spmd.clone.sunk | while | flops 819335168 | bytes 80586552 | solution.py:104
  111.2 17.2 %all_gather.13 = bf16[8192,10]{0,1:T(8,128)(2,1)S(1)} all-gather(bf16[2048,10]{0,1:T(8,128)(2,1)S(1)} %copy-done.8), channel_id=1, replica_groups=mesh['narrow'=4,'wide'=8] {'narrow'}, dimensions={0}, use_global_device_ids=true | all-gather | bytes 204800 | tf_op jit(solution)/shard_map/all_gather | solution.py:112
  142.5 40.2 %all-reduce.16 = (f32[8192]{0:T(1024)S(1)}, f32[]{:T(128)}, f32[8192]{0:T(1024)S(1)}) all-reduce(f32[8192]{0:T(1024)S(1)} %bitcast.234, f32[]{:T(128)} %get-tuple-element.659, f32[8192]{0:T(1024)S(1)} %bitcast.235), channel_id=1, replica_groups=mesh['narrow'=4,'wide'=8] {'wide'}, use_global_device_ids=true, to_apply=%region_3.4 | all-reduce | flops 16385 | bytes 131080 | tf_op jit(solution)/shard_map/psum | solution.py:117
  182.7 12.5 %all-reduce.17 = (f32[8192]{0:T(1024)S(1)}, f32[]{:T(128)}, f32[8192]{0:T(1024)S(1)}) all-reduce(f32[8192]{0:T(1024)S(1)} %get-tuple-element.631, f32[]{:T(128)} %get-tuple-element.632, f32[8192]{0:T(1024)S(1)} %get-tuple-element.633), channel_id=1, replica_groups=mesh['narrow'=4,'wide'=8] {'narrow'}, use_global_device_ids=true, to_apply=%region_4.5 | all-reduce | flops 16385 | bytes 131080 | tf_op jit(solution)/shard_map/psum | solution.py:116
  195.2 67.6 %all-reduce.15.cloned.1.call-done = (f32[8192]{0:T(1024)}, f32[8192]{0:T(1024)}, f32[10]{0:T(128)}) async-done(((f32[8192]{0:T(1024)}, f32[8192]{0:T(1024)}, f32[10]{0:T(128)}), (f32[8192]{0:T(1024)}, f32[8192]{0:T(1024)}, f32[10]{0:T(128)})) %all-reduce.15.cloned.1.call-update) | async-done | bytes 65592 | tf_op jit(solution)/shard_map/psum | solution.py:126
  269.3 9.2 %copy.36 = bf16[2,32,8192]{1,0,2:T(2,128)(2,1)} copy(bf16[2,32,8192]{2,1,0:T(8,128)(2,1)} %add_convert_fusion) | data formatting | bytes 2097152 | tf_op jit(solution)/shard_map/convert_element_type | solution.py:11
  278.5 6.4 reshape.80
  291.1 12.9 %all-to-all-done.1 = bf16[4,2,65536]{2,1,0:T(2,128)(2,1)} async-done(((bf16[4,2,65536]{2,1,0:T(2,128)(2,1)}), bf16[4,2,65536]{2,1,0:T(2,128)(2,1)}, u32[]{:S(2)}, u32[]{:S(2)}) %all-to-all-start.1) | async-done | bytes 1048608 | tf_op jit(solution)/shard_map/all_to_all | solution.py:130
  309.2 6.6 convert_bitcast_fusion
  315.8 11.7 %copy.37 = f32[4,2,32,2048]{3,2,1,0:T(8,128)} copy(f32[4,2,32,2048]{2,1,3,0:T(2,128)} %convert_bitcast_fusion) | data formatting | bytes 4194304 | tf_op jit(solution)/shard_map/convert_element_type | solution.py:134
  328.6 62.1 %while.60 = (s32[]{:T(128)}, f32[32,2048]{1,0:T(8,128)S(1)}, bf16[8,32,2048]{2,1,0:T(8,128)(2,1)}, f32[2048]{0:T(1024)S(1)}, f32[8,32,2048]{2,1,0:T(8,128)}, /*i...) while((s32[]{:T(128)}, f32[32,2048]{1,0:T(8,128)S(1)}, ...), condition=%wide.region_16.17_spmd.clone, body=%wide.region_15.16_spmd.clone.sunk | while | flops 269158400 | bytes 10387604 | solution.py:42
  330.3 6.0 convolution_add_fusion.7
  338.1 6.0 convolution_add_fusion.7
  345.9 6.0 convolution_add_fusion.7
  353.6 6.0 convolution_add_fusion.7
  361.4 6.0 convolution_add_fusion.7
  369.2 6.0 convolution_add_fusion.7
  384.7 6.0 convolution_add_fusion.7
  390.7 7.4 fusion.17
  399.2 62.0 %while.61 = (s32[]{:T(128)}, f32[32,2048]{1,0:T(8,128)S(1)}, bf16[8,32,2048]{2,1,0:T(8,128)(2,1)}, f32[2048]{0:T(1024)S(1)}, f32[8,32,2048]{2,1,0:T(8,128)}, /*i...) while((s32[]{:T(128)}, f32[32,2048]{1,0:T(8,128)S(1)}, ...), condition=%wide.region_18.19_spmd.clone, body=%wide.region_17.18_spmd.clone.sunk | while | flops 269158400 | bytes 10387604 | solution.py:42
  400.9 6.0 convolution_add_fusion.8
  408.7 6.0 convolution_add_fusion.8
  416.5 6.0 convolution_add_fusion.8
  473.6 8.0 %reshape.84 = bf16[8,2,32768]{2,1,0:T(2,128)(2,1)} reshape(bf16[2048,8,32]{2,1,0:T(8,128)(2,1)} %bitcast.204) | data formatting | bytes 2097152
  491.2 7.8 reshape.82
  499.1 36.5 %all-to-all-done.3 = bf16[8,2,32768]{2,1,0:T(2,128)(2,1)} async-done(((bf16[8,2,32768]{2,1,0:T(2,128)(2,1)}), bf16[8,2,32768]{2,1,0:T(2,128)(2,1)}, u32[]{:S(2)}, u32[]{:S(2)}) %all-to-all-start.3) | async-done | bytes 1048608 | tf_op jit(solution)/shard_map/all_to_all | solution.py:136
  539.1 83.1 %all_gather.15 = bf16[8,256,100]{2,1,0:T(8,128)(2,1)} all-gather(bf16[8,32,100]{2,1,0:T(8,128)(2,1)S(1)} %get-tuple-element.1060), channel_id=1, replica_groups=mesh['narrow'=4,'wide'=8] {'wide'}, dimensions={1}, use_global_device_ids=true | all-gather | bytes 460800 | tf_op jit(solution)/shard_map/all_gather | solution.py:152
  626.8 7.1 reshape.85
  649.3 13.2 %copy.41 = bf16[8,32,8,256]{3,1,2,0:T(8,128)(2,1)S(1)} copy(bf16[8,32,8,256]{1,0,3,2:T(8,128)(2,1)} %bitcast.206) | data formatting | bytes 2097152 | tf_op jit(solution)/shard_map/all_to_all | solution.py:150
  663.6 19.6 %fusion.23 = f32[1,2048,256]{2,1,0:T(8,128)} fusion(bf16[8,256,256]{2,1,0:T(8,128)(2,1)S(1)} %bitcast.212, bf16[7,256,2048]{2,0,1:T(8,128)(2,1)} %bitcast.239), kind=kOutput, calls=%fused_computation.47 | convolution fusion | flops 1879048192 | bytes 10485760 | tf_op jit(solution)/shard_map/tbr,tbq->rq/dot_general | solution.py:51
  683.2 79.5 %all-gather.5.cloned.1.call-done = bf16[8,256,2048]{2,0,1:T(8,128)(2,1)} async-done(((bf16[8,32,2048]{2,0,1:T(8,128)(2,1)}), bf16[8,256,2048]{2,0,1:T(8,128)(2,1)}) %all-gather.5.cloned.1.call-update) | async-done | bytes 8388624 | tf_op jit(solution)/shard_map/all_gather | solution.py:138
  762.8 19.8 %fusion.26 = f32[1,2048,256]{2,1,0:T(8,128)} fusion(bf16[8,256,256]{2,1,0:T(8,128)(2,1)S(1)} %bitcast.230, bf16[7,256,2048]{2,0,1:T(8,128)(2,1)} %bitcast.240), kind=kOutput, calls=%fused_computation.48 | convolution fusion | flops 1879048192 | bytes 10485760 | tf_op jit(solution)/shard_map/tbr,tbq->rq/dot_general | solution.py:51
  (273 shorter events, 252.2 us)
Async XLA Ops:
  12.6 6.0 slice-start
  12.6 6.0 slice-start.1
  24.3 6.0 slice-start
  24.3 6.0 slice-start.1
  36.1 6.0 slice-start
  36.1 6.0 slice-start.1
  59.6 6.0 slice-start
  59.6 6.0 slice-start.1
  71.4 6.0 slice-start
  71.4 6.0 slice-start.1
  83.1 6.0 slice-start
  83.2 6.0 slice-start.1
  94.9 6.0 slice-start
  94.9 6.0 slice-start.1
  106.7 21.7 %copy-start.10 = (s32[32,8]{0,1:T(8,128)S(1)}, s32[32,8]{0,1:T(8,128)}, u32[]{:S(2)}) copy-start(s32[32,8]{0,1:T(8,128)} %param.21) | copy-start | bytes 3076
  106.7 21.7 %copy-start.11 = (s32[32]{0:T(128)S(1)}, s32[32]{0:T(128)}, u32[]{:S(2)}) copy-start(s32[32]{0:T(128)} %param.23) | copy-start | bytes 388
  106.7 21.7 %copy-start.12 = (s32[32]{0:T(128)S(1)}, s32[32]{0:T(128)}, u32[]{:S(2)}) copy-start(s32[32]{0:T(128)} %param.22) | copy-start | bytes 388
  106.7 23.0 %all-to-all-start = ((bf16[8,32,2048]{2,1,0:T(8,128)(2,1)}), bf16[8,32,2048]{2,1,0:T(8,128)(2,1)}, u32[]{:S(2)}, u32[]{:S(2)}) async-start(bf16[8,32,2048]{2,1,0:T(8,128)(2,1)} %get-tuple-element.423), calls=%async_computation | async-start | bytes 2097152 | tf_op jit(solution)/shard_map/all_to_all | solution.py:111
  111.1 151.6 %all-reduce.15.cloned.1.call-start = ((), (), s32[]{:S(2)}) async-start(), calls=%async_computation.8 | async-start | bytes 132096 | tf_op jit(solution)/shard_map/psum | solution.py:126
  111.2 28.9 %copy-start.7 = (bf16[32,8,10]{0,2,1:T(8,128)(2,1)}, bf16[32,8,10]{0,2,1:T(8,128)(2,1)S(1)}, u32[]{:S(2)}) copy-start(bf16[32,8,10]{0,2,1:T(8,128)(2,1)S(1)} %copy.74) | copy-start | bytes 15364
  284.9 19.1 %all-to-all-start.1 = ((bf16[4,2,65536]{2,1,0:T(2,128)(2,1)}), bf16[4,2,65536]{2,1,0:T(2,128)(2,1)}, u32[]{:S(2)}, u32[]{:S(2)}) async-start(bf16[4,2,65536]{2,1,0:T(2,128)(2,1)} %reshape.80), calls=%async_computation.1 | async-start | bytes 2097152 | tf_op jit(solution)/shard_map/all_to_all | solution.py:130
  289.1 334.5 %all-reduce.13.cloned.1.call-start = ((), (), s32[]{:S(2)}) async-start(), calls=%async_computation.7 | async-start | bytes 1048576 | tf_op jit(solution)/shard_map/psum | solution.py:126
  291.1 334.1 %all-reduce.11.cloned.1.call-start = ((), (), s32[]{:S(2)}) async-start(), calls=%async_computation.4 | async-start | bytes 262144 | tf_op jit(solution)/shard_map/psum | solution.py:149
  463.6 200.0 %all-gather.3.cloned.1.call-start = ((), (), s32[]{:S(2)}) async-start(), calls=%async_computation.5 | async-start | bytes 9437184 | tf_op jit(solution)/shard_map/all_gather | solution.py:151
  466.4 296.3 %all-gather.5.cloned.1.call-start = ((), (), s32[]{:S(2)}) async-start(), calls=%async_computation.6 | async-start | bytes 9437184 | tf_op jit(solution)/shard_map/all_gather | solution.py:138
  481.5 54.0 %all-to-all-start.3 = ((bf16[8,2,32768]{2,1,0:T(2,128)(2,1)}), bf16[8,2,32768]{2,1,0:T(2,128)(2,1)}, u32[]{:S(2)}, u32[]{:S(2)}) async-start(bf16[8,2,32768]{2,1,0:T(2,128)(2,1)} %reshape.84), calls=%async_computation.3 | async-start | bytes 2097152 | tf_op jit(solution)/shard_map/all_to_all | solution.py:136
  499.1 123.2 %copy-start.13 = (f32[10]{0:T(128)S(1)}, f32[10]{0:T(128)}, u32[]{:S(2)}) copy-start(f32[10]{0:T(128)} %param.31) | copy-start | bytes 124
  535.5 109.2 %all-to-all-start.2 = ((bf16[8,2,32768]{2,1,0:T(2,128)(2,1)}), bf16[8,2,32768]{2,1,0:T(2,128)(2,1)S(1)}, u32[]{:S(2)}, u32[]{:S(2)}) async-start(bf16[8,2,32768]{2,1,0:T(2,128)(2,1)} %reshape.82), calls=%async_computation.2 | async-start | bytes 2097152 | tf_op jit(solution)/shard_map/all_to_all | solution.py:150
  649.3 13.2 %copy-start.4 = (bf16[8,256,100]{2,1,0:T(8,128)(2,1)S(1)}, bf16[8,256,100]{2,1,0:T(8,128)(2,1)}, u32[]{:S(2)}) copy-start(bf16[8,256,100]{2,1,0:T(8,128)(2,1)} %all_gather.15) | copy-start | bytes 1228804
  663.6 99.2 %copy-start.6 = (bf16[8,32,8,256]{3,1,2,0:T(8,128)(2,1)S(1)}, bf16[8,32,8,256]{3,1,2,0:T(8,128)(2,1)}, u32[]{:S(2)}) copy-start(bf16[8,32,8,256]{3,1,2,0:T(8,128)(2,1)} %copy.43) | copy-start | bytes 3145732
  762.8 19.8 %copy-start.5 = (bf16[8,32,8,256]{3,0,1,2:T(8,128)(2,1)S(1)}, bf16[8,32,8,256]{3,0,1,2:T(8,128)(2,1)}, u32[]{:S(2)}) copy-start(bf16[8,32,8,256]{3,0,1,2:T(8,128)(2,1)} %copy.52) | copy-start | bytes 3145732
  762.8 19.8 %copy-start.14 = (bf16[8,256,2048]{2,0,1:T(8,128)(2,1)S(1)}, bf16[8,256,2048]{2,0,1:T(8,128)(2,1)}, u32[]{:S(2)}) copy-start(bf16[8,256,2048]{2,0,1:T(8,128)(2,1)} %all-gather.3.cloned.1.call-done) | copy-start | bytes 25165828
  (25 other events, 82.6 us)
Sparse Core Ops, SparseCore 0:
  142.6 120.0 all-reduce.14
  295.2 129.0 all-reduce.12
  463.7 31.2 all-reduce.10
Sparse Core Ops, SparseCore 1:
  466.7 170.6 all-gather.2
  639.4 123.3 all-gather.4
